TPU v7x, 512 devices: a whole 4x8x8 slice. The times are simulated.
512 devices in a mesh: grp: 16 (over y_lo, z), dev: 32 (over x, y_hi, core).
Axes of the slice: x: 4, y: 8 (y_hi: 4, y_lo: 2; y = y_hi * 2 + y_lo), z: 8, core: 2. Of those that a mesh axis runs over, the one named last changes fastest.
Arguments:
- samples: bfloat16 [262144, 768], P(('grp', 'dev')), may hold values from -8 to 8
- targets: bfloat16 [262144, 768], P(('grp', 'dev')), may hold values from -8 to 8
- row_slot: int32 [262144], P(('grp', 'dev')), may hold values from 0 to 63, as said below
- hot_group: int32 [32], P('dev'), may hold values from 0 to 15
- anchor: bfloat16 [512, 768, 768], P(('grp', 'dev')), may hold values from -0.21875 to 0.21875
Outputs:
- rotation: bfloat16 [512, 768, 768], P(('grp', 'dev'))
Inputs may be any that keep to these rules, and one draw needn't show every extreme that they name: `row_slot`: on each device at most 16 rows carry the same value; in every group one value is carried by exactly 16 rows on every device of the group.
All inputs are finite; a program needn't handle non-finite values.
Results may differ from a plain program's by a relative error of at most 0.027.
Values may be sent and summed in bfloat16 or wider, within the bound.
A program may use at most 128 MiB of HBM per device.

v0:
```python
import math

import jax
import jax.numpy as jnp
from jax import lax
from jax.sharding import PartitionSpec as P

ITERS = 2


first_coef = 3.4445
third_coef = -4.775
fifth_coef = 2.0315


def polar_factor(matrix, features):
    rounded = matrix.astype(jnp.bfloat16)
    gram_matrix = jnp.dot(rounded, rounded.T, preferred_element_type=jnp.float32)
    norm_value = jnp.sqrt(jnp.sum(gram_matrix * gram_matrix) + 1e-06)
    iterate = (matrix / jnp.sqrt(norm_value)).astype(jnp.bfloat16)
    square = (gram_matrix / norm_value).astype(jnp.bfloat16)
    update = iterate.astype(jnp.float32)
    for sweep in range(ITERS):
        if sweep > 0:
            square = jnp.dot(iterate, iterate.T, preferred_element_type=jnp.float32).astype(
                jnp.bfloat16
            )
        squared_twice = jnp.dot(square, square, preferred_element_type=jnp.float32)
        blend = (third_coef * square.astype(jnp.float32) + fifth_coef * squared_twice).astype(
            jnp.bfloat16
        )
        update = first_coef * iterate.astype(jnp.float32) + jnp.dot(
            blend, iterate, preferred_element_type=jnp.float32
        )
        if sweep + 1 < ITERS:
            iterate = update.astype(jnp.bfloat16)
    return (math.sqrt(features) * update).astype(jnp.bfloat16)


def accumulate(row_values, row_targets, features):
    flat_values = row_values.reshape(-1, features)
    flat_targets = row_targets.reshape(-1, features)
    return jnp.dot(flat_targets.T, flat_values, preferred_element_type=jnp.float32)


def reduce_hot(hot_values, hot_targets, features):
    summed_hot = lax.psum(
        accumulate(hot_values, hot_targets, features).astype(jnp.bfloat16), "grp"
    ).astype(jnp.float32)
    return summed_hot


def shards(samples, targets, row_slot, hot_group, anchor):
    columns = lax.axis_size("dev")
    row_count = samples.shape[0]
    features = samples.shape[1]
    capacity = row_count // columns
    buckets = 2 * columns
    labels = jnp.arange(buckets, dtype=jnp.int32)
    member = (row_slot[:, None] == labels[None, :]).astype(jnp.int32)
    rank_in = jnp.sum(jnp.cumsum(member, axis=0) * member, axis=1) - 1
    position = row_slot * capacity + rank_in
    owner_row = (
        jnp.zeros((buckets * capacity,), jnp.int32)
        .at[position]
        .set(jnp.arange(row_count, dtype=jnp.int32) + 1)
    )
    filled = owner_row > 0
    source = jnp.maximum(owner_row - 1, 0)
    zero_value = jnp.zeros((), jnp.bfloat16)
    sent_values = jnp.where(filled[:, None], jnp.take(samples, source, axis=0), zero_value).reshape(
        2, columns, capacity, features
    )
    sent_targets = jnp.where(
        filled[:, None], jnp.take(targets, source, axis=0), zero_value
    ).reshape(2, columns, capacity, features)
    received_values, received_targets = (
        lax.all_to_all(sent_values, "dev", split_axis=1, concat_axis=1, tiled=True),
        lax.all_to_all(sent_targets, "dev", split_axis=1, concat_axis=1, tiled=True),
    )
    summed_hot = reduce_hot(received_values[1], received_targets[1], features)
    cold_sum = accumulate(received_values[0], received_targets[0], features)
    owned = lax.axis_index("grp") == hot_group[0]
    weight = math.sqrt(features * row_count) / 2.0
    matrix = cold_sum + jnp.where(owned, summed_hot, jnp.zeros_like(summed_hot))
    matrix = matrix + weight * anchor[0].astype(jnp.float32)
    return polar_factor(matrix, features)[None]


def solution(mesh):
    return jax.shard_map(
        shards,
        mesh=mesh,
        in_specs=(
            P(("grp", "dev"), None),
            P(("grp", "dev"), None),
            P(("grp", "dev")),
            P("dev"),
            P(("grp", "dev"), None, None),
        ),
        out_specs=P(("grp", "dev"), None, None),
        check_vma=False,
    )
```

profile of v0, /device:TPU:2, one launch (start us, length us, event | category | flops | bytes accessed | tf_op | source)
XLA Modules:
  0.0 293.7 jit_solution(403609045787172942)
XLA Ops:
  6.5 0.8 fusion.6
  7.3 1.2 reduce-window.6
  8.5 0.2 slice_reduce_fusion
  8.8 0.8 fusion.5
  9.6 0.7 compare_select_fusion
  10.3 2.4 scatter_custom_fusion
  12.8 4.0 %gather_fusion.1 = bf16[1024,768]{1,0:T(8,128)(2,1)S(1)} fusion(bf16[512,768]{1,0:T(8,128)(2,1)S(1)} %copy-done, s32[1024]{0:T(1024)S(1)} %fusion.8), kind=kCustom, calls=%fused_computation.1.clone | custom fusion | bytes 3149824 | tf_op jit(solution)/shard_map/jit(_take)/gather | solution.py:71
  16.8 5.2 %gather_fusion = bf16[1024,768]{1,0:T(8,128)(2,1)} fusion(bf16[512,768]{1,0:T(8,128)(2,1)S(1)} %copy-done.1, s32[1024]{0:T(1024)S(1)} %fusion.8), kind=kCustom, calls=%fused_computation.clone | custom fusion | bytes 3149824 | tf_op jit(solution)/shard_map/jit(_take)/gather | solution.py:75
  22.0 2.9 select_select_fusion.1
  24.9 1.3 copy.12
  26.2 10.3 %all-to-all-start.1 = ((bf16[2,32,16,768]{3,2,0,1:T(8,128)(2,1)}), bf16[2,32,16,768]{3,2,0,1:T(8,128)(2,1)S(1)}, u32[]{:S(2)}, u32[]{:S(2)}) async-start(bf16[2,32,16,768]{3,2,0,1:T(8,128)(2,1)} %copy.12), calls=%async_computation.1 | async-start | bytes 3145728 | tf_op jit(solution)/shard_map/all_to_all | solution.py:78
  36.5 2.8 copy.10
  39.3 36.0 %all-to-all-done.1 = bf16[2,32,16,768]{3,2,0,1:T(8,128)(2,1)S(1)} async-done(((bf16[2,32,16,768]{3,2,0,1:T(8,128)(2,1)}), bf16[2,32,16,768]{3,2,0,1:T(8,128)(2,1)S(1)}, u32[]{:S(2)}, u32[]{:S(2)}) %all-to-all-start.1) | async-done | bytes 1572896 | tf_op jit(solution)/shard_map/all_to_all | solution.py:78
  75.2 7.3 %all-to-all-start = ((bf16[2,32,16,768]{3,2,0,1:T(8,128)(2,1)}), bf16[2,32,16,768]{3,2,0,1:T(8,128)(2,1)}, u32[]{:S(2)}, u32[]{:S(2)}) async-start(bf16[2,32,16,768]{3,2,0,1:T(8,128)(2,1)} %copy.10), calls=%async_computation | async-start | bytes 3145728 | tf_op jit(solution)/shard_map/all_to_all | solution.py:79
  82.5 1.0 fusion.16
  83.6 36.8 %all-to-all-done = bf16[2,32,16,768]{3,2,0,1:T(8,128)(2,1)} async-done(((bf16[2,32,16,768]{3,2,0,1:T(8,128)(2,1)}), bf16[2,32,16,768]{3,2,0,1:T(8,128)(2,1)}, u32[]{:S(2)}, u32[]{:S(2)}) %all-to-all-start) | async-done | bytes 1572896 | tf_op jit(solution)/shard_map/all_to_all | solution.py:79
  120.4 1.5 fusion.15
  121.9 1.9 bitcast_convert_fusion
  124.5 145.2 %all-reduce.2.cloned.1.call-done = bf16[768,768]{1,0:T(8,128)(2,1)} async-done(((bf16[768,768]{1,0:T(8,128)(2,1)}), bf16[768,768]{1,0:T(8,128)(2,1)}) %all-reduce.2.cloned.1.call-update) | async-done | bytes 1179664 | tf_op jit(solution)/shard_map/psum | solution.py:47
  269.7 2.7 bitcast_add_fusion
  272.4 1.9 multiply_reduce_fusion
  275.1 5.6 %add_convert_fusion.1 = bf16[768,768]{1,0:T(8,128)(2,1)} fusion(f32[768,768]{1,0:T(8,128)} %copy-done.3, f32[]{:T(128)S(6)} %sqrt.7, f32[768,768]{1,0:T(8,128)S(1)} %get-tuple-element.15, f32[]{:T(128)S(6)} %sqrt.6), kind=kOutput, calls=%fused_computation.8 | convolution fusion | flops 1821966336 | bytes 5898248 | tf_op jit(solution)/shard_map/dot_general | solution.py:32
  280.7 2.9 convolution_convert_fusion
  283.6 3.2 %fusion = bf16[1,768,768]{2,1,0:T(8,128)(2,1)} fusion(bf16[768,768]{1,0:T(8,128)(2,1)S(1)} %copy-done.4, bf16[768,768]{1,0:T(8,128)(2,1)S(1)} %convolution_convert_fusion), kind=kOutput, calls=%fused_computation.16 | convolution fusion | flops 1817837568 | bytes 3538944 | tf_op jit(solution)/shard_map/dot_general | solution.py:32
  (16 shorter events, 0.1 us)
Async XLA Ops:
  6.5 6.2 %copy-start = (bf16[512,768]{1,0:T(8,128)(2,1)S(1)}, bf16[512,768]{1,0:T(8,128)(2,1)}, u32[]{:S(2)}) copy-start(bf16[512,768]{1,0:T(8,128)(2,1)} %param.7) | copy-start | bytes 2359300
  12.8 4.0 %copy-start.1 = (bf16[512,768]{1,0:T(8,128)(2,1)S(1)}, bf16[512,768]{1,0:T(8,128)(2,1)}, u32[]{:S(2)}) copy-start(bf16[512,768]{1,0:T(8,128)(2,1)} %param.8) | copy-start | bytes 2359300
  26.2 49.0 %all-to-all-start.1 = ((bf16[2,32,16,768]{3,2,0,1:T(8,128)(2,1)}), bf16[2,32,16,768]{3,2,0,1:T(8,128)(2,1)S(1)}, u32[]{:S(2)}, u32[]{:S(2)}) async-start(bf16[2,32,16,768]{3,2,0,1:T(8,128)(2,1)} %copy.12), calls=%async_computation.1 | async-start | bytes 3145728 | tf_op jit(solution)/shard_map/all_to_all | solution.py:78
  75.2 45.2 %all-to-all-start = ((bf16[2,32,16,768]{3,2,0,1:T(8,128)(2,1)}), bf16[2,32,16,768]{3,2,0,1:T(8,128)(2,1)}, u32[]{:S(2)}, u32[]{:S(2)}) async-start(bf16[2,32,16,768]{3,2,0,1:T(8,128)(2,1)} %copy.10), calls=%async_computation | async-start | bytes 3145728 | tf_op jit(solution)/shard_map/all_to_all | solution.py:79
  82.5 187.2 %all-reduce.2.cloned.1.call-start = ((), (), s32[]{:S(2)}) async-start(), calls=%async_computation.2 | async-start | bytes 2359296 | tf_op jit(solution)/shard_map/psum | solution.py:47
  83.5 38.3 %copy-start.2 = (bf16[1,32,16,768]{3,2,0,1:T(8,128)(2,1)S(1)}, bf16[1,32,16,768]{3,2,0,1:T(8,128)(2,1)}, u32[]{:S(2)}) copy-start(bf16[1,32,16,768]{3,2,0,1:T(8,128)(2,1)} %get-tuple-element.9) | copy-start | bytes 2359300
  272.4 1.9 copy-start.3
  280.7 2.9 copy-start.4
Sparse Core Ops, SparseCore 0:
  124.0 145.6 all-reduce.1
where the time goes:
time: 294 us
  waiting for transfers between devices  218 us (74%)
  local copies, waits for them, and re-layouts  18.5 us (6%)
  matrix products  18.3 us (6%)
  starting transfers between devices  17.6 us (6%)
  between operations  14.9 us (5%)
  other arithmetic  6.42 us (2%)
    psum x1, waiting for transfers between devices, reduce_hot(): lax.psum(accumulate(hot_values, hot_targets, features).astype(jnp.bfloat1...  145 us
    all_to_all x1, waiting for transfers between devices, shards(): lax.all_to_all(sent_targets, 'dev', split_axis=1, concat_axis=1, tiled=True)  36.8 us
    all_to_all x1, waiting for transfers between devices, shards(): lax.all_to_all(sent_values, 'dev', split_axis=1, concat_axis=1, tiled=True)  36 us
    all_to_all x1, starting transfers between devices, shards(): lax.all_to_all(sent_values, 'dev', split_axis=1, concat_axis=1, tiled=True)  10.3 us
    dot_general x2, matrix products, polar_factor(): jnp.dot(blend, iterate, preferred_element_type=jnp.float32)  8.78 us
    all_to_all x1, starting transfers between devices, shards(): lax.all_to_all(sent_targets, 'dev', split_axis=1, concat_axis=1, tiled=True)  7.26 us
  transfers between devices with their start and end apart: 3, of which 3 were waited for; matrix products, arithmetic and copies ran while one was open for 1% of the time, Pallas kernels for 0%

commit v1 on v0

v1 whole, which is shorter than its diff:
```python
import functools
import math

import jax
import jax.numpy as jnp
from jax import lax
from jax.experimental import pallas as pl
from jax.experimental.pallas import tpu as pltpu
from jax.sharding import PartitionSpec as P

MESH = pl.DeviceIdType.MESH
ITERS = 2
first_coef = 3.4445
third_coef = -4.775
fifth_coef = 2.0315

NX, NY, NZ, NC = 4, 8, 8, 2
COLUMNS = 32
CAP = 16
D = 768
PIECE = D // NZ
HALF = PIECE // 2


def device_at(x, y, z, c):
    return (lax.rem(y, 2) * NZ + z, x * 8 + lax.div(y, 2) * 2 + c)


def exchange(
    slot_ref, samples_ref, targets_ref, hot_ref, cold_ref,
    send_hot, send_cold, recv_hot, recv_cold, hot_sum, rs_first, rs_own, rs_in, partial, moved,
    hot_ssem, hot_rsem, cold_ssem, cold_rsem, rs_ssem, rs_rsem, mv_ssem, mv_rsem, ag_ssem, ag_rsem,
):
    grp, dev = lax.axis_index("grp"), lax.axis_index("dev")
    y_lo, z = lax.div(grp, NZ), lax.rem(grp, NZ)
    x, y_hi, c = lax.div(dev, 8), lax.rem(lax.div(dev, 2), 4), lax.rem(dev, 2)
    y = 2 * y_hi + y_lo
    wrap_x = lambda v: lax.rem(v + NX, NX)
    wrap_y = lambda v: lax.rem(v + NY, NY)
    wrap_z = lambda v: lax.rem(v + NZ, NZ)

    def offsets(r):
        return lax.div(r, 8), lax.rem(lax.div(r, 2), 4), lax.rem(r, 2)

    def hot_step(q, core):
        return q - 4 * lax.div(2 * q + core, 5)

    def hot_target(r):
        dx, q, dc = offsets(r)
        core = lax.rem(c + dc, 2)
        row = wrap_y(y + hot_step(q, core))
        col = wrap_x(x + dx) * 8 + lax.rem(row, 4) * 2 + core
        return device_at(wrap_x(x + dx), row, z, core), col

    def hot_source(r):
        dx, q, dc = offsets(r)
        return device_at(wrap_x(x - dx), wrap_y(y - hot_step(q, c)), z, lax.rem(c + dc, 2))

    def cold_target(r):
        dx, q, dc = offsets(r)
        core, hi = lax.rem(c + dc, 2), lax.rem(y_hi + q, 4)
        col = wrap_x(x + dx) * 8 + hi * 2 + core
        return (grp, col), col

    def cold_source(r):
        dx, q, dc = offsets(r)
        return (grp, wrap_x(x - dx) * 8 + lax.rem(y_hi + 4 - q, 4) * 2 + lax.rem(c + dc, 2))

    z_ids = (device_at(x, y, wrap_z(z - 1), c), device_at(x, y, wrap_z(z + 1), c))
    move_rows = tuple(2 * lax.rem(y, 4) + t for t in range(2))
    from_rows = tuple(y_hi + 4 * s for s in range(2))

    barrier = pltpu.get_barrier_semaphore()

    def greet(r, carry):
        pl.semaphore_signal(barrier, inc=1, device_id=hot_source(r), device_id_type=MESH)
        pl.semaphore_signal(barrier, inc=1, device_id=cold_source(r), device_id_type=MESH)
        return carry

    lax.fori_loop(1, COLUMNS, greet, 0)
    for other in z_ids:
        pl.semaphore_signal(barrier, inc=1, device_id=other, device_id_type=MESH)
    for row in from_rows:
        @pl.when(row != y)
        def _():
            pl.semaphore_signal(barrier, inc=1, device_id=device_at(x, row, z, c), device_id_type=MESH)

    slot = slot_ref[...]
    rows = slot.shape[1]
    member = (lax.broadcasted_iota(jnp.int32, (2 * COLUMNS, rows), 0) == slot).astype(jnp.float32)
    before = (
        lax.broadcasted_iota(jnp.int32, (rows, rows), 0) < lax.broadcasted_iota(jnp.int32, (rows, rows), 1)
    ).astype(jnp.float32).astype(jnp.bfloat16)
    count = jnp.dot(member.astype(jnp.bfloat16), before, preferred_element_type=jnp.float32)
    rank = jnp.sum(count * member, axis=0, keepdims=True)
    place = slot * CAP + rank.astype(jnp.int32)

    def sort_into(out, base):
        pick = (
            (lax.broadcasted_iota(jnp.int32, (COLUMNS * CAP, rows), 0) + base) == place
        ).astype(jnp.float32).astype(jnp.bfloat16)
        for ref, lane in ((samples_ref, 0), (targets_ref, D)):
            picked = jnp.dot(pick, ref[...], preferred_element_type=jnp.float32).astype(jnp.bfloat16)
            out[:, :, lane:lane + D] = picked.reshape(COLUMNS, CAP, D)

    sort_into(send_hot, COLUMNS * CAP)

    elsewhere = 2 - lax.div(y + 1, NY) - lax.div(NY - y, NY)
    pl.semaphore_wait(barrier, 2 * (COLUMNS - 1) + 2 + elsewhere)

    def send_rows(target, out, into, ssem, rsem, first=1, last=COLUMNS):
        def body(r, carry):
            where, col = target(r)
            pltpu.make_async_remote_copy(
                src_ref=out.at[col], dst_ref=into.at[r], send_sem=ssem, recv_sem=rsem,
                device_id=where, device_id_type=MESH,
            ).start()
            return carry
        lax.fori_loop(first, last, body, 0)

    def wait_rows(ref, sem):
        many = ref.at[pl.ds(1, COLUMNS - 1)]
        pltpu.make_async_copy(many, many, sem).wait()

    def outer_sum(ref):
        both = ref[...].reshape(COLUMNS * CAP, 2 * D)
        return lax.dot_general(
            both[:, D:], both[:, :D], (((0,), (0,)), ((), ())), preferred_element_type=jnp.float32
        )

    send_rows(hot_target, send_hot, recv_hot, hot_ssem, hot_rsem)
    recv_hot[0] = send_hot[hot_target(0)[1]]
    sort_into(send_cold, 0)
    recv_cold[0] = send_cold[dev]
    wait_rows(send_hot, hot_ssem)
    started = [1]

    def drip(n):
        first, last = started[0], min(started[0] + n, COLUMNS)
        if first < last:
            send_rows(cold_target, send_cold, recv_cold, cold_ssem, cold_rsem, first, last)
        started[0] = last

    drip(3)
    wait_rows(recv_hot, hot_rsem)
    hot_sum[...] = outer_sum(recv_hot)

    def rows_of(piece, sub):
        return pl.ds(pl.multiple_of(piece * PIECE + sub * HALF, CAP), HALF)

    def rs_piece(way, k):
        return wrap_z(z + (k - 5 if way == 0 else 5 - k) + NZ)

    def rs_send(way, k, sub, src):
        copy = pltpu.make_async_remote_copy(
            src_ref=src, dst_ref=rs_in.at[way, k - 1, pl.ds(sub * HALF, HALF)],
            send_sem=rs_ssem.at[way, k - 1, sub], recv_sem=rs_rsem.at[way, k - 1, sub],
            device_id=z_ids[way], device_id_type=MESH,
        )
        copy.start()
        pending.append(copy)

    def rs_wait(way, k, sub):
        drip(1)
        part = rs_in.at[way, k - 1, pl.ds(sub * HALF, HALF)]
        pltpu.make_async_copy(part, part, rs_rsem.at[way, k - 1, sub]).wait()
        return part

    pending = []
    for way in range(2):
        rs_first[way] = hot_sum[rows_of(rs_piece(way, 1), way), :].astype(jnp.bfloat16)
        rs_send(way, 1, way, rs_first.at[way])
    for way in range(2):
        rs_own[way] = hot_sum[rows_of(rs_piece(way, 2), 1 - way), :].astype(jnp.bfloat16)
        rs_send(way, 2, 1 - way, rs_own.at[way])
    for k in range(2, 5):
        for turn in range(2):
            for way in range(2):
                sub = 1 - way if turn == 0 else way
                if k == 2 and turn == 0:
                    continue
                part = rs_wait(way, k - 1, sub)
                part[...] = (
                    part[...].astype(jnp.float32) + hot_sum[rows_of(rs_piece(way, k), sub), :]
                ).astype(jnp.bfloat16)
                rs_send(way, k, sub, part)

    for sub in range(2):
        total = hot_sum[rows_of(z, sub), :]
        for way in range(2):
            total = total + rs_wait(way, 4, sub)[...].astype(jnp.float32)
        half = pl.ds(sub * HALF, HALF)
        partial[half, :] = total.astype(jnp.bfloat16)
        for t, row in enumerate(move_rows):
            slot_no = lax.div(y, 4)

            @pl.when(row != y)
            def _():
                pltpu.make_async_remote_copy(
                    src_ref=partial.at[half], dst_ref=moved.at[slot_no, half],
                    send_sem=mv_ssem.at[t, sub], recv_sem=mv_rsem.at[slot_no, sub],
                    device_id=device_at(x, row, z, c), device_id_type=MESH,
                ).start()

            @pl.when(row == y)
            def _():
                pltpu.make_async_copy(
                    partial.at[half], moved.at[slot_no, half], mv_rsem.at[slot_no, sub]
                ).start()

    def ag_copy(way, k, sub, piece):
        part = hot_ref.at[rows_of(piece, sub)]
        return pltpu.make_async_remote_copy(
            src_ref=part, dst_ref=part, send_sem=ag_ssem.at[way, k - 1, sub],
            recv_sem=ag_rsem.at[way, k - 1, sub], device_id=z_ids[way], device_id_type=MESH,
        )

    def ag_send(way, k, sub):
        piece = wrap_z(z + (k - 1 if way == 0 else 1 - k))
        copy = ag_copy(way, k, sub, piece)
        copy.start()
        pending.append(copy)

    for sub in range(2):
        half = pl.ds(sub * HALF, HALF)
        total = jnp.zeros((HALF, D), jnp.float32)
        for s in range(2):
            part = moved.at[s, half]
            drip(1)
            pltpu.make_async_copy(part, part, mv_rsem.at[s, sub]).wait()
            total = total + part[...].astype(jnp.float32)
        hot_ref[rows_of(z, sub), :] = total.astype(jnp.bfloat16)
        for way in range(2):
            ag_send(way, 1, sub)
    for k in range(1, 5):
        for sub in range(2):
            for way in range(2):
                if k == 4 and sub != way:
                    continue
                drip(1)
                ag_copy(way, k, sub, wrap_z(z + (k if way == 0 else -k))).wait_recv()
                if k < 3 or (k == 3 and sub == way):
                    ag_send(way, k + 1, sub)

    drip(COLUMNS)
    wait_rows(recv_cold, cold_rsem)
    cold_ref[...] = outer_sum(recv_cold)

    wait_rows(send_cold, cold_ssem)
    for copy in pending:
        copy.wait_send()
    for sub in range(2):
        for t, row in enumerate(move_rows):
            @pl.when(row != y)
            def _():
                part = partial.at[pl.ds(sub * HALF, HALF)]
                pltpu.make_async_copy(part, part, mv_ssem.at[t, sub]).wait()


def polar(weight, owned_ref, cold_ref, hot_ref, anchor_ref, out_ref):
    hot = hot_ref[...].astype(jnp.float32)
    matrix = cold_ref[...] + jnp.where(owned_ref[0] > 0, hot, jnp.zeros_like(hot))
    matrix = matrix + weight * anchor_ref[...].astype(jnp.float32)
    rounded = matrix.astype(jnp.bfloat16)
    last = (((1,), (1,)), ((), ()))
    gram = lax.dot_general(rounded, rounded, last, preferred_element_type=jnp.float32)
    norm = jnp.sqrt(jnp.sum(gram * gram) + 1e-06)
    iterate = (matrix / jnp.sqrt(norm)).astype(jnp.bfloat16)
    square = (gram / norm).astype(jnp.bfloat16)
    update = None
    for sweep in range(ITERS):
        if sweep > 0:
            square = lax.dot_general(iterate, iterate, last, preferred_element_type=jnp.float32)
            square = square.astype(jnp.bfloat16)
        twice = jnp.dot(square, square, preferred_element_type=jnp.float32)
        blend = (third_coef * square.astype(jnp.float32) + fifth_coef * twice).astype(jnp.bfloat16)
        update = first_coef * iterate.astype(jnp.float32) + jnp.dot(
            blend, iterate, preferred_element_type=jnp.float32
        )
        iterate = update.astype(jnp.bfloat16)
    out_ref[...] = (math.sqrt(D) * update).astype(jnp.bfloat16)


def shards(samples, targets, row_slot, hot_group, anchor):
    rows = samples.shape[0]
    vmem = pl.BlockSpec(memory_space=pltpu.VMEM)
    dma = pltpu.SemaphoreType.DMA
    hot, cold = pl.pallas_call(
        exchange,
        out_shape=(
            jax.ShapeDtypeStruct((D, D), jnp.bfloat16),
            jax.ShapeDtypeStruct((D, D), jnp.float32),
        ),
        in_specs=[vmem] * 3,
        out_specs=(vmem, vmem),
        scratch_shapes=[
            pltpu.VMEM((COLUMNS, CAP, 2 * D), jnp.bfloat16),
            pltpu.VMEM((COLUMNS, CAP, 2 * D), jnp.bfloat16),
            pltpu.VMEM((COLUMNS, CAP, 2 * D), jnp.bfloat16),
            pltpu.VMEM((COLUMNS, CAP, 2 * D), jnp.bfloat16),
            pltpu.VMEM((D, D), jnp.float32),
            pltpu.VMEM((2, HALF, D), jnp.bfloat16),
            pltpu.VMEM((2, HALF, D), jnp.bfloat16),
            pltpu.VMEM((2, 4, PIECE, D), jnp.bfloat16),
            pltpu.VMEM((PIECE, D), jnp.bfloat16),
            pltpu.VMEM((2, PIECE, D), jnp.bfloat16),
            dma, dma, dma, dma,
            dma((2, 4, 2)), dma((2, 4, 2)),
            dma((2, 2)), dma((2, 2)),
            dma((2, 4, 2)), dma((2, 4, 2)),
        ],
        compiler_params=pltpu.CompilerParams(
            collective_id=0, has_side_effects=True, vmem_limit_bytes=48 << 20
        ),
    )(row_slot.reshape(1, rows), samples, targets)
    owned = (lax.axis_index("grp") == hot_group).astype(jnp.int32)
    weight = math.sqrt(D * rows) / 2.0
    rotation = pl.pallas_call(
        functools.partial(polar, weight),
        out_shape=jax.ShapeDtypeStruct((D, D), jnp.bfloat16),
        in_specs=[pl.BlockSpec(memory_space=pltpu.SMEM)] + [vmem] * 3,
        out_specs=vmem,
        compiler_params=pltpu.CompilerParams(vmem_limit_bytes=48 << 20),
    )(owned, cold, hot, anchor[0])
    return rotation[None]


def solution(mesh):
    return jax.shard_map(
        shards,
        mesh=mesh,
        in_specs=(
            P(("grp", "dev"), None),
            P(("grp", "dev"), None),
            P(("grp", "dev")),
            P("dev"),
            P(("grp", "dev"), None, None),
        ),
        out_specs=P(("grp", "dev"), None, None),
        check_vma=False,
    )
```

time: 294 us -> 106 us (0.36)
  the two profiles are of different devices: /device:TPU:2 before, /device:TPU:13 now
where the time goes in v1:
time: 106 us; the launch traced here: 105 us
  Pallas kernels  102 us (96%)
  local copies, waits for them, and re-layouts  2.94 us (3%)
    pallas_call x1, Pallas kernels, shards(): pl.pallas_call(exchange, out_shape=(jax.ShapeDtypeStruct((D, D), jnp.bflo...  93.2 us
    pallas_call x1, Pallas kernels, shards(): pl.pallas_call(functools.partial(polar, weight), out_shape=jax.ShapeDtype...  8.46 us
    unnamed x8, local copies, waits for them, and re-layouts  2.94 us

profile of v1, /device:TPU:13, one launch (start us, length us, event | category | flops | bytes accessed | tf_op | source)
XLA Modules:
  0.0 105.4 jit_solution(17299814562172095617)
XLA Ops:
  0.0 0.0 copy-start
  0.8 0.0 copy-start.1
  0.8 1.1 %copy-done.1 = bf16[512,768]{1,0:T(8,128)(2,1)S(1)} copy-done((bf16[512,768]{1,0:T(8,128)(2,1)S(1)}, bf16[512,768]{1,0:T(8,128)(2,1)}, u32[]{:S(2)}) %copy-start.1) | copy-done | bytes 786456
  1.9 0.0 copy-start.2
  1.9 1.1 %copy-done.2 = bf16[512,768]{1,0:T(8,128)(2,1)S(1)} copy-done((bf16[512,768]{1,0:T(8,128)(2,1)S(1)}, bf16[512,768]{1,0:T(8,128)(2,1)}, u32[]{:S(2)}) %copy-start.2) | copy-done | bytes 786456
  3.0 0.0 copy-start.3
  3.0 0.7 copy-done.3
  3.7 93.2 %shard_map.55 = (bf16[768,768]{1,0:T(8,128)(2,1)S(1)}, f32[768,768]{1,0:T(8,128)S(1)}) custom-call(s32[1,512]{1,0:T(1,128)S(1)} %bitcast.5, bf16[512,768]{1,0:T(8,128)(2,1)S(1)} %copy-done.1, bf16[512,768]{1,0:T(8,128)(2,1)S(1)} %copy-done.2), custom_call_target="tpu_custom_call" | custom-call | tf_op jit(solution)/shard_map/pallas_call | solution.py:288
  96.9 0.0 copy-done
  96.9 8.5 %shard_map.56 = bf16[768,768]{1,0:T(8,128)(2,1)} custom-call(s32[1]{0:T(128)S(6)} %convert_element_type.3.owned_ref, f32[768,768]{1,0:T(8,128)S(1)} %get-tuple-element.7.cold_ref, bf16[768,768]{1,0:T(8,128)(2,1)S(1)} %get-tuple-element.8.hot_ref, bf16[768,768]{1,0:T(8,128)(2,1)S(1)} %bitcast.4), custom_call_target="tpu_custom_call" | custom-call | tf_op jit(solution)/shard_map/pallas_call | solution.py:318
Async XLA Ops:
  0.0 96.9 %copy-start = (bf16[1,768,768]{2,1,0:T(8,128)(2,1)S(1)}, bf16[1,768,768]{2,1,0:T(8,128)(2,1)}, u32[]{:S(2)}) copy-start(bf16[1,768,768]{2,1,0:T(8,128)(2,1)} %param.9) | copy-start | bytes 3538948
  0.8 1.1 %copy-start.1 = (bf16[512,768]{1,0:T(8,128)(2,1)S(1)}, bf16[512,768]{1,0:T(8,128)(2,1)}, u32[]{:S(2)}) copy-start(bf16[512,768]{1,0:T(8,128)(2,1)} %samples_ref.1) | copy-start | bytes 2359300
  1.9 1.1 %copy-start.2 = (bf16[512,768]{1,0:T(8,128)(2,1)S(1)}, bf16[512,768]{1,0:T(8,128)(2,1)}, u32[]{:S(2)}) copy-start(bf16[512,768]{1,0:T(8,128)(2,1)} %targets_ref.1) | copy-start | bytes 2359300
  3.0 0.7 copy-start.3

commit v2 on v1

--- a/solution.py
+++ b/solution.py
@@ -19,7 +19,9 @@
 CAP = 16
 D = 768
 PIECE = D // NZ
-HALF = PIECE // 2
+SUBS = 2
+SUB = PIECE // SUBS
+FIRST, SECOND, PACE = 0, 3, 1
 
 
 def device_at(x, y, z, c):
@@ -27,14 +29,23 @@
 
 
 def exchange(
-    slot_ref, samples_ref, targets_ref, hot_ref, cold_ref,
+    weight, slot_hbm, samples_hbm, targets_hbm, anchor_hbm, hot_ref, base_ref,
+    slot_ref, samples_ref, targets_ref, anchor_ref,
     send_hot, send_cold, recv_hot, recv_cold, hot_sum, rs_first, rs_own, rs_in, partial, moved,
-    hot_ssem, hot_rsem, cold_ssem, cold_rsem, rs_ssem, rs_rsem, mv_ssem, mv_rsem, ag_ssem, ag_rsem,
+    in_sems, hot_ssem, hot_rsem, cold_ssem, cold_rsem, rs_ssem, rs_rsem, mv_ssem, mv_rsem, ag_ssem, ag_rsem,
 ):
     grp, dev = lax.axis_index("grp"), lax.axis_index("dev")
     y_lo, z = lax.div(grp, NZ), lax.rem(grp, NZ)
     x, y_hi, c = lax.div(dev, 8), lax.rem(lax.div(dev, 2), 4), lax.rem(dev, 2)
     y = 2 * y_hi + y_lo
+    loads = [
+        pltpu.make_async_copy(src, dst, in_sems.at[i])
+        for i, (src, dst) in enumerate(
+            ((slot_hbm, slot_ref), (samples_hbm, samples_ref), (targets_hbm, targets_ref), (anchor_hbm, anchor_ref))
+        )
+    ]
+    for load in loads:
+        load.start()
     wrap_x = lambda v: lax.rem(v + NX, NX)
     wrap_y = lambda v: lax.rem(v + NY, NY)
     wrap_z = lambda v: lax.rem(v + NZ, NZ)
@@ -85,6 +96,7 @@
         def _():
             pl.semaphore_signal(barrier, inc=1, device_id=device_at(x, row, z, c), device_id_type=MESH)
 
+    loads[0].wait()
     slot = slot_ref[...]
     rows = slot.shape[1]
     member = (lax.broadcasted_iota(jnp.int32, (2 * COLUMNS, rows), 0) == slot).astype(jnp.float32)
@@ -103,6 +115,8 @@
             picked = jnp.dot(pick, ref[...], preferred_element_type=jnp.float32).astype(jnp.bfloat16)
             out[:, :, lane:lane + D] = picked.reshape(COLUMNS, CAP, D)
 
+    loads[1].wait()
+    loads[2].wait()
     sort_into(send_hot, COLUMNS * CAP)
 
     elsewhere = 2 - lax.div(y + 1, NY) - lax.div(NY - y, NY)
@@ -128,32 +142,45 @@
             both[:, D:], both[:, :D], (((0,), (0,)), ((), ())), preferred_element_type=jnp.float32
         )
 
+    started = [1]
+    events = [0]
+
+    def start_cold(n):
+        first, last = started[0], min(started[0] + n, COLUMNS)
+        if first < last:
+            send_rows(cold_target, send_cold, recv_cold, cold_ssem, cold_rsem, first, last)
+        started[0] = last
+
+    def pace():
+        events[0] += 1
+        if events[0] % PACE == 0:
+            start_cold(1)
+
     send_rows(hot_target, send_hot, recv_hot, hot_ssem, hot_rsem)
     recv_hot[0] = send_hot[hot_target(0)[1]]
     sort_into(send_cold, 0)
     recv_cold[0] = send_cold[dev]
+    start_cold(FIRST)
     wait_rows(send_hot, hot_ssem)
-    started = [1]
-
-    def drip(n):
-        first, last = started[0], min(started[0] + n, COLUMNS)
-        if first < last:
-            send_rows(cold_target, send_cold, recv_cold, cold_ssem, cold_rsem, first, last)
-        started[0] = last
-
-    drip(3)
+    start_cold(SECOND)
     wait_rows(recv_hot, hot_rsem)
     hot_sum[...] = outer_sum(recv_hot)
 
-    def rows_of(piece, sub):
-        return pl.ds(pl.multiple_of(piece * PIECE + sub * HALF, CAP), HALF)
+    def rows_of(piece, sub, subs=1):
+        return pl.ds(pl.multiple_of(piece * PIECE + sub * SUB, CAP), subs * SUB)
+
+    far = (range(SUBS // 2), range(SUBS // 2, SUBS))
+    order = (tuple(far[1]) + tuple(far[0]), tuple(far[0]) + tuple(far[1]))
 
     def rs_piece(way, k):
         return wrap_z(z + (k - 5 if way == 0 else 5 - k) + NZ)
 
+    def rs_slot(way, k, sub):
+        return rs_in.at[way, k - 1, pl.ds(sub * SUB, SUB)]
+
     def rs_send(way, k, sub, src):
         copy = pltpu.make_async_remote_copy(
-            src_ref=src, dst_ref=rs_in.at[way, k - 1, pl.ds(sub * HALF, HALF)],
+            src_ref=src, dst_ref=rs_slot(way, k, sub),
             send_sem=rs_ssem.at[way, k - 1, sub], recv_sem=rs_rsem.at[way, k - 1, sub],
             device_id=z_ids[way], device_id_type=MESH,
         )
@@ -161,23 +188,25 @@
         pending.append(copy)
 
     def rs_wait(way, k, sub):
-        drip(1)
-        part = rs_in.at[way, k - 1, pl.ds(sub * HALF, HALF)]
+        pace()
+        part = rs_slot(way, k, sub)
         pltpu.make_async_copy(part, part, rs_rsem.at[way, k - 1, sub]).wait()
         return part
 
     pending = []
-    for way in range(2):
-        rs_first[way] = hot_sum[rows_of(rs_piece(way, 1), way), :].astype(jnp.bfloat16)
-        rs_send(way, 1, way, rs_first.at[way])
-    for way in range(2):
-        rs_own[way] = hot_sum[rows_of(rs_piece(way, 2), 1 - way), :].astype(jnp.bfloat16)
-        rs_send(way, 2, 1 - way, rs_own.at[way])
+    for k, kept in ((1, rs_first), (2, rs_own)):
+        for way in range(2):
+            subs = far[way] if k == 1 else far[1 - way]
+            kept[way] = hot_sum[rows_of(rs_piece(way, k), subs[0], SUBS // 2), :].astype(jnp.bfloat16)
+        for i in range(SUBS // 2):
+            for way in range(2):
+                subs = far[way] if k == 1 else far[1 - way]
+                rs_send(way, k, subs[i], kept.at[way, pl.ds(i * SUB, SUB)])
     for k in range(2, 5):
-        for turn in range(2):
+        for turn in range(SUBS):
             for way in range(2):
-                sub = 1 - way if turn == 0 else way
-                if k == 2 and turn == 0:
+                sub = order[way][turn]
+                if k == 2 and sub not in far[way]:
                     continue
                 part = rs_wait(way, k - 1, sub)
                 part[...] = (
@@ -185,19 +214,18 @@
                 ).astype(jnp.bfloat16)
                 rs_send(way, k, sub, part)
 
-    for sub in range(2):
+    slot_no = lax.div(y, 4)
+    for sub in range(SUBS):
         total = hot_sum[rows_of(z, sub), :]
         for way in range(2):
             total = total + rs_wait(way, 4, sub)[...].astype(jnp.float32)
-        half = pl.ds(sub * HALF, HALF)
-        partial[half, :] = total.astype(jnp.bfloat16)
+        part = pl.ds(sub * SUB, SUB)
+        partial[part, :] = total.astype(jnp.bfloat16)
         for t, row in enumerate(move_rows):
-            slot_no = lax.div(y, 4)
-
             @pl.when(row != y)
             def _():
                 pltpu.make_async_remote_copy(
-                    src_ref=partial.at[half], dst_ref=moved.at[slot_no, half],
+                    src_ref=partial.at[part], dst_ref=moved.at[slot_no, part],
                     send_sem=mv_ssem.at[t, sub], recv_sem=mv_rsem.at[slot_no, sub],
                     device_id=device_at(x, row, z, c), device_id_type=MESH,
                 ).start()
@@ -205,7 +233,7 @@
             @pl.when(row == y)
             def _():
                 pltpu.make_async_copy(
-                    partial.at[half], moved.at[slot_no, half], mv_rsem.at[slot_no, sub]
+                    partial.at[part], moved.at[slot_no, part], mv_rsem.at[slot_no, sub]
                 ).start()
 
     def ag_copy(way, k, sub, piece):
@@ -216,57 +244,56 @@
         )
 
     def ag_send(way, k, sub):
-        piece = wrap_z(z + (k - 1 if way == 0 else 1 - k))
-        copy = ag_copy(way, k, sub, piece)
+        copy = ag_copy(way, k, sub, wrap_z(z + (k - 1 if way == 0 else 1 - k)))
         copy.start()
         pending.append(copy)
 
-    for sub in range(2):
-        half = pl.ds(sub * HALF, HALF)
-        total = jnp.zeros((HALF, D), jnp.float32)
+    for sub in range(SUBS):
+        part = pl.ds(sub * SUB, SUB)
+        total = jnp.zeros((SUB, D), jnp.float32)
         for s in range(2):
-            part = moved.at[s, half]
-            drip(1)
-            pltpu.make_async_copy(part, part, mv_rsem.at[s, sub]).wait()
-            total = total + part[...].astype(jnp.float32)
+            pace()
+            come = moved.at[s, part]
+            pltpu.make_async_copy(come, come, mv_rsem.at[s, sub]).wait()
+            total = total + come[...].astype(jnp.float32)
         hot_ref[rows_of(z, sub), :] = total.astype(jnp.bfloat16)
         for way in range(2):
             ag_send(way, 1, sub)
     for k in range(1, 5):
-        for sub in range(2):
+        for sub in range(SUBS):
             for way in range(2):
-                if k == 4 and sub != way:
+                if k == 4 and sub not in far[way]:
                     continue
-                drip(1)
+                pace()
                 ag_copy(way, k, sub, wrap_z(z + (k if way == 0 else -k))).wait_recv()
-                if k < 3 or (k == 3 and sub == way):
+                if k < 3 or (k == 3 and sub in far[way]):
                     ag_send(way, k + 1, sub)
 
-    drip(COLUMNS)
+    start_cold(COLUMNS)
+    loads[3].wait()
     wait_rows(recv_cold, cold_rsem)
-    cold_ref[...] = outer_sum(recv_cold)
+    base_ref[...] = outer_sum(recv_cold) + weight * anchor_ref[...].astype(jnp.float32)
 
     wait_rows(send_cold, cold_ssem)
     for copy in pending:
         copy.wait_send()
-    for sub in range(2):
+    for sub in range(SUBS):
         for t, row in enumerate(move_rows):
             @pl.when(row != y)
             def _():
-                part = partial.at[pl.ds(sub * HALF, HALF)]
+                part = partial.at[pl.ds(sub * SUB, SUB)]
                 pltpu.make_async_copy(part, part, mv_ssem.at[t, sub]).wait()
 
 
-def polar(weight, owned_ref, cold_ref, hot_ref, anchor_ref, out_ref):
+def polar(owned_ref, base_ref, hot_ref, out_ref):
     hot = hot_ref[...].astype(jnp.float32)
-    matrix = cold_ref[...] + jnp.where(owned_ref[0] > 0, hot, jnp.zeros_like(hot))
-    matrix = matrix + weight * anchor_ref[...].astype(jnp.float32)
+    matrix = base_ref[...] + jnp.where(owned_ref[0] > 0, hot, jnp.zeros_like(hot))
     rounded = matrix.astype(jnp.bfloat16)
     last = (((1,), (1,)), ((), ()))
     gram = lax.dot_general(rounded, rounded, last, preferred_element_type=jnp.float32)
     norm = jnp.sqrt(jnp.sum(gram * gram) + 1e-06)
-    iterate = (matrix / jnp.sqrt(norm)).astype(jnp.bfloat16)
-    square = (gram / norm).astype(jnp.bfloat16)
+    iterate = (matrix * (1.0 / jnp.sqrt(norm))).astype(jnp.bfloat16)
+    square = (gram * (1.0 / norm)).astype(jnp.bfloat16)
     update = None
     for sweep in range(ITERS):
         if sweep > 0:
@@ -285,43 +312,51 @@
     rows = samples.shape[0]
     vmem = pl.BlockSpec(memory_space=pltpu.VMEM)
     dma = pltpu.SemaphoreType.DMA
-    hot, cold = pl.pallas_call(
-        exchange,
+    hbm = pl.BlockSpec(memory_space=pltpu.HBM)
+    weight = math.sqrt(D * rows) / 2.0
+    hot, base = pl.pallas_call(
+        functools.partial(exchange, weight),
         out_shape=(
             jax.ShapeDtypeStruct((D, D), jnp.bfloat16),
             jax.ShapeDtypeStruct((D, D), jnp.float32),
         ),
-        in_specs=[vmem] * 3,
+        in_specs=[hbm] * 4,
         out_specs=(vmem, vmem),
         scratch_shapes=[
+            pltpu.VMEM((1, rows), jnp.int32),
+            pltpu.VMEM((rows, D), jnp.bfloat16),
+            pltpu.VMEM((rows, D), jnp.bfloat16),
+            pltpu.VMEM((D, D), jnp.bfloat16),
             pltpu.VMEM((COLUMNS, CAP, 2 * D), jnp.bfloat16),
             pltpu.VMEM((COLUMNS, CAP, 2 * D), jnp.bfloat16),
             pltpu.VMEM((COLUMNS, CAP, 2 * D), jnp.bfloat16),
             pltpu.VMEM((COLUMNS, CAP, 2 * D), jnp.bfloat16),
             pltpu.VMEM((D, D), jnp.float32),
-            pltpu.VMEM((2, HALF, D), jnp.bfloat16),
-            pltpu.VMEM((2, HALF, D), jnp.bfloat16),
+            pltpu.VMEM((2, PIECE // 2, D), jnp.bfloat16),
+            pltpu.VMEM((2, PIECE // 2, D), jnp.bfloat16),
             pltpu.VMEM((2, 4, PIECE, D), jnp.bfloat16),
             pltpu.VMEM((PIECE, D), jnp.bfloat16),
             pltpu.VMEM((2, PIECE, D), jnp.bfloat16),
-            dma, dma, dma, dma,
-            dma((2, 4, 2)), dma((2, 4, 2)),
-            dma((2, 2)), dma((2, 2)),
-            dma((2, 4, 2)), dma((2, 4, 2)),
+            dma((4,)), dma, dma, dma, dma,
+            dma((2, 4, SUBS)), dma((2, 4, SUBS)),
+            dma((2, SUBS)), dma((2, SUBS)),
+            dma((2, 4, SUBS)), dma((2, 4, SUBS)),
         ],
         compiler_params=pltpu.CompilerParams(
-            collective_id=0, has_side_effects=True, vmem_limit_bytes=48 << 20
+            collective_id=0, has_side_effects=True, vmem_limit_bytes=24 << 20
         ),
-    )(row_slot.reshape(1, rows), samples, targets)
+    )(*(
+        pltpu.with_memory_space_constraint(a, pltpu.HBM)
+        for a in (row_slot.reshape(1, rows), samples, targets, anchor[0])
+    ))
     owned = (lax.axis_index("grp") == hot_group).astype(jnp.int32)
-    weight = math.sqrt(D * rows) / 2.0
     rotation = pl.pallas_call(
-        functools.partial(polar, weight),
+        polar,
         out_shape=jax.ShapeDtypeStruct((D, D), jnp.bfloat16),
-        in_specs=[pl.BlockSpec(memory_space=pltpu.SMEM)] + [vmem] * 3,
+        in_specs=[pl.BlockSpec(memory_space=pltpu.SMEM), vmem, vmem],
         out_specs=vmem,
-        compiler_params=pltpu.CompilerParams(vmem_limit_bytes=48 << 20),
-    )(owned, cold, hot, anchor[0])
+        compiler_params=pltpu.CompilerParams(vmem_limit_bytes=24 << 20),
+    )(owned, base, hot)
     return rotation[None]
 
 

time: 106 us -> 103 us (0.972)
  local copies, waits for them, and re-layouts: 2.94 us -> 0 us
    unnamed x8 -> x0, local copies, waits for them, and re-layouts: 2.94 us -> none
where the time goes in v2:
time: 103 us; the launch traced here: 102 us
  Pallas kernels  102 us (99%)
    pallas_call x1, Pallas kernels, shards(): pl.pallas_call(functools.partial(exchange, weight), out_shape=(jax.ShapeD...  93.3 us
    pallas_call x1, Pallas kernels, shards(): pl.pallas_call(polar, out_shape=jax.ShapeDtypeStruct((D, D), jnp.bfloat16...  8.39 us

profile of v2, /device:TPU:13, one launch (start us, length us, event | category | flops | bytes accessed | tf_op | source)
XLA Modules:
  0.0 102.4 jit_solution(13860724958543869253)
XLA Ops:
  0.7 93.3 %shard_map.55 = (bf16[768,768]{1,0:T(8,128)(2,1)S(1)}, f32[768,768]{1,0:T(8,128)S(1)}) custom-call(s32[1,512]{1,0:T(1,128)} %bitcast.5, bf16[512,768]{1,0:T(8,128)(2,1)} %samples_hbm.1, bf16[512,768]{1,0:T(8,128)(2,1)} %targets_hbm.1, bf16[768,768]{1,0:T(8,128)(2,1)} %bitcast.4), custom_call_target="tpu_custom_call" | custom-call | tf_op jit(solution)/shard_map/pallas_call | solution.py:317
  94.0 8.4 %shard_map.56 = bf16[768,768]{1,0:T(8,128)(2,1)} custom-call(s32[1]{0:T(128)S(6)} %convert_element_type.3.owned_ref, f32[768,768]{1,0:T(8,128)S(1)} %get-tuple-element.7.base_ref, bf16[768,768]{1,0:T(8,128)(2,1)S(1)} %get-tuple-element.8.hot_ref), custom_call_target="tpu_custom_call" | custom-call | tf_op jit(solution)/shard_map/pallas_call | solution.py:353

commit v3 on v2

--- a/solution.py
+++ b/solution.py
@@ -21,7 +21,7 @@
 PIECE = D // NZ
 SUBS = 2
 SUB = PIECE // SUBS
-FIRST, SECOND, PACE = 0, 3, 1
+FIRST, SECOND, PACE = 0, 6, 1
 
 
 def device_at(x, y, z, c):
@@ -53,6 +53,13 @@
     def offsets(r):
         return lax.div(r, 8), lax.rem(lax.div(r, 2), 4), lax.rem(r, 2)
 
+    def gray(v):
+        return v + lax.div(v, 2) * (1 - 2 * lax.rem(v, 2))
+
+    def ordered(i):
+        u, v = lax.rem(lax.div(i, 4), 4), lax.rem(i, 4)
+        return 8 * gray(lax.rem(u + v, 4)) + 2 * gray(v) + lax.div(i, 16)
+
     def hot_step(q, core):
         return q - 4 * lax.div(2 * q + core, 5)
 
@@ -123,7 +130,8 @@
     pl.semaphore_wait(barrier, 2 * (COLUMNS - 1) + 2 + elsewhere)
 
     def send_rows(target, out, into, ssem, rsem, first=1, last=COLUMNS):
-        def body(r, carry):
+        def body(i, carry):
+            r = ordered(i)
             where, col = target(r)
             pltpu.make_async_remote_copy(
                 src_ref=out.at[col], dst_ref=into.at[r], send_sem=ssem, recv_sem=rsem,
@@ -260,6 +268,11 @@
         for way in range(2):
             ag_send(way, 1, sub)
     for k in range(1, 5):
+        if k == 4:
+            start_cold(COLUMNS)
+            loads[3].wait()
+            wait_rows(recv_cold, cold_rsem)
+            base_ref[...] = outer_sum(recv_cold) + weight * anchor_ref[...].astype(jnp.float32)
         for sub in range(SUBS):
             for way in range(2):
                 if k == 4 and sub not in far[way]:
@@ -268,11 +281,6 @@
                 ag_copy(way, k, sub, wrap_z(z + (k if way == 0 else -k))).wait_recv()
                 if k < 3 or (k == 3 and sub in far[way]):
                     ag_send(way, k + 1, sub)
-
-    start_cold(COLUMNS)
-    loads[3].wait()
-    wait_rows(recv_cold, cold_rsem)
-    base_ref[...] = outer_sum(recv_cold) + weight * anchor_ref[...].astype(jnp.float32)
 
     wait_rows(send_cold, cold_ssem)
     for copy in pending:

time: 103 us -> 95.4 us (0.926)
  the two profiles are of different devices: /device:TPU:13 before, /device:TPU:48 now
where the time goes in v3:
time: 95.4 us; the launch traced here: 95.3 us
  Pallas kernels  94.6 us (99%)
    pallas_call x1, Pallas kernels, shards(): pl.pallas_call(functools.partial(exchange, weight), out_shape=(jax.ShapeD...  86.2 us
    pallas_call x1, Pallas kernels, shards(): pl.pallas_call(polar, out_shape=jax.ShapeDtypeStruct((D, D), jnp.bfloat16...  8.39 us

profile of v3, /device:TPU:48, one launch (start us, length us, event | category | flops | bytes accessed | tf_op | source)
XLA Modules:
  0.0 95.3 jit_solution(15798460215364225494)
XLA Ops:
  0.7 86.2 %shard_map.55 = (bf16[768,768]{1,0:T(8,128)(2,1)S(1)}, f32[768,768]{1,0:T(8,128)S(1)}) custom-call(s32[1,512]{1,0:T(1,128)} %bitcast.5, bf16[512,768]{1,0:T(8,128)(2,1)} %samples_hbm.1, bf16[512,768]{1,0:T(8,128)(2,1)} %targets_hbm.1, bf16[768,768]{1,0:T(8,128)(2,1)} %bitcast.4), custom_call_target="tpu_custom_call" | custom-call | tf_op jit(solution)/shard_map/pallas_call | solution.py:325
  86.9 8.4 %shard_map.56 = bf16[768,768]{1,0:T(8,128)(2,1)} custom-call(s32[1]{0:T(128)S(6)} %convert_element_type.3.owned_ref, f32[768,768]{1,0:T(8,128)S(1)} %get-tuple-element.7.base_ref, bf16[768,768]{1,0:T(8,128)(2,1)S(1)} %get-tuple-element.8.hot_ref), custom_call_target="tpu_custom_call" | custom-call | tf_op jit(solution)/shard_map/pallas_call | solution.py:361

commit v4 on v3

--- a/solution.py
+++ b/solution.py
@@ -10,6 +10,7 @@
 
 MESH = pl.DeviceIdType.MESH
 ITERS = 2
+ROWS = 256
 first_coef = 3.4445
 third_coef = -4.775
 fifth_coef = 2.0315
@@ -298,22 +299,38 @@
     matrix = base_ref[...] + jnp.where(owned_ref[0] > 0, hot, jnp.zeros_like(hot))
     rounded = matrix.astype(jnp.bfloat16)
     last = (((1,), (1,)), ((), ()))
-    gram = lax.dot_general(rounded, rounded, last, preferred_element_type=jnp.float32)
-    norm = jnp.sqrt(jnp.sum(gram * gram) + 1e-06)
+    blocks = [slice(i, i + ROWS) for i in range(0, D, ROWS)]
+    gram = [
+        lax.dot_general(rounded[rows], rounded, last, preferred_element_type=jnp.float32) for rows in blocks
+    ]
+    norm = jnp.sqrt(sum(jnp.sum(part * part) for part in gram) + 1e-06)
     iterate = (matrix * (1.0 / jnp.sqrt(norm))).astype(jnp.bfloat16)
-    square = (gram * (1.0 / norm)).astype(jnp.bfloat16)
-    update = None
+    scale = 1.0 / norm
+    square = jnp.concatenate([(part * scale).astype(jnp.bfloat16) for part in gram], axis=0)
     for sweep in range(ITERS):
         if sweep > 0:
-            square = lax.dot_general(iterate, iterate, last, preferred_element_type=jnp.float32)
-            square = square.astype(jnp.bfloat16)
-        twice = jnp.dot(square, square, preferred_element_type=jnp.float32)
-        blend = (third_coef * square.astype(jnp.float32) + fifth_coef * twice).astype(jnp.bfloat16)
-        update = first_coef * iterate.astype(jnp.float32) + jnp.dot(
-            blend, iterate, preferred_element_type=jnp.float32
-        )
-        iterate = update.astype(jnp.bfloat16)
-    out_ref[...] = (math.sqrt(D) * update).astype(jnp.bfloat16)
+            square = jnp.concatenate(
+                [
+                    lax.dot_general(
+                        iterate[rows], iterate, last, preferred_element_type=jnp.float32
+                    ).astype(jnp.bfloat16)
+                    for rows in blocks
+                ],
+                axis=0,
+            )
+        made = []
+        for rows in blocks:
+            twice = jnp.dot(square[rows], square, preferred_element_type=jnp.float32)
+            blend = (third_coef * square[rows].astype(jnp.float32) + fifth_coef * twice).astype(jnp.bfloat16)
+            update = first_coef * iterate[rows].astype(jnp.float32) + jnp.dot(
+                blend, iterate, preferred_element_type=jnp.float32
+            )
+            if sweep + 1 < ITERS:
+                made.append(update.astype(jnp.bfloat16))
+            else:
+                out_ref[rows, :] = (math.sqrt(D) * update).astype(jnp.bfloat16)
+        if made:
+            iterate = jnp.concatenate(made, axis=0)
 
 
 def shards(samples, targets, row_slot, hot_group, anchor):

time: 95.4 us -> 94.8 us (level)
  no operation moved by 1% of the time
where the time goes in v4:
time: 94.8 us; the launch traced here: 94.7 us
  Pallas kernels  94 us (99%)
    pallas_call x1, Pallas kernels, shards(): pl.pallas_call(functools.partial(exchange, weight), out_shape=(jax.ShapeD...  86.2 us
    pallas_call x1, Pallas kernels, shards(): pl.pallas_call(polar, out_shape=jax.ShapeDtypeStruct((D, D), jnp.bfloat16...  7.79 us

profile of v4, /device:TPU:48, one launch (start us, length us, event | category | flops | bytes accessed | tf_op | source)
XLA Modules:
  0.0 94.7 jit_solution(12618153486059720567)
XLA Ops:
  0.7 86.2 %shard_map.55 = (bf16[768,768]{1,0:T(8,128)(2,1)S(1)}, f32[768,768]{1,0:T(8,128)S(1)}) custom-call(s32[1,512]{1,0:T(1,128)} %bitcast.5, bf16[512,768]{1,0:T(8,128)(2,1)} %samples_hbm.1, bf16[512,768]{1,0:T(8,128)(2,1)} %targets_hbm.1, bf16[768,768]{1,0:T(8,128)(2,1)} %bitcast.4), custom_call_target="tpu_custom_call" | custom-call | tf_op jit(solution)/shard_map/pallas_call | solution.py:342
  86.9 7.8 %shard_map.56 = bf16[768,768]{1,0:T(8,128)(2,1)} custom-call(s32[1]{0:T(128)S(6)} %convert_element_type.3.owned_ref, f32[768,768]{1,0:T(8,128)S(1)} %get-tuple-element.7.base_ref, bf16[768,768]{1,0:T(8,128)(2,1)S(1)} %get-tuple-element.8.hot_ref), custom_call_target="tpu_custom_call" | custom-call | tf_op jit(solution)/shard_map/pallas_call | solution.py:378

commit v5 on v4

--- a/solution.py
+++ b/solution.py
@@ -96,7 +96,7 @@
         pl.semaphore_signal(barrier, inc=1, device_id=cold_source(r), device_id_type=MESH)
         return carry
 
-    lax.fori_loop(1, COLUMNS, greet, 0)
+    lax.fori_loop(1, COLUMNS, greet, 0, unroll=True)
     for other in z_ids:
         pl.semaphore_signal(barrier, inc=1, device_id=other, device_id_type=MESH)
     for row in from_rows:
@@ -139,7 +139,7 @@
                 device_id=where, device_id_type=MESH,
             ).start()
             return carry
-        lax.fori_loop(first, last, body, 0)
+        lax.fori_loop(first, last, body, 0, unroll=True)
 
     def wait_rows(ref, sem):
         many = ref.at[pl.ds(1, COLUMNS - 1)]

time: 94.8 us -> 94 us (level)
  no operation moved by 1% of the time
where the time goes in v5:
time: 94 us; the launch traced here: 93.8 us
  Pallas kernels  93.1 us (99%)
    pallas_call x1, Pallas kernels, shards(): pl.pallas_call(functools.partial(exchange, weight), out_shape=(jax.ShapeD...  85.4 us
    pallas_call x1, Pallas kernels, shards(): pl.pallas_call(polar, out_shape=jax.ShapeDtypeStruct((D, D), jnp.bfloat16...  7.8 us

profile of v5, /device:TPU:48, one launch (start us, length us, event | category | flops | bytes accessed | tf_op | source)
XLA Modules:
  0.0 93.8 jit_solution(4135597954681968967)
XLA Ops:
  0.7 85.4 %shard_map.55 = (bf16[768,768]{1,0:T(8,128)(2,1)S(1)}, f32[768,768]{1,0:T(8,128)S(1)}) custom-call(s32[1,512]{1,0:T(1,128)} %bitcast.5, bf16[512,768]{1,0:T(8,128)(2,1)} %samples_hbm.1, bf16[512,768]{1,0:T(8,128)(2,1)} %targets_hbm.1, bf16[768,768]{1,0:T(8,128)(2,1)} %bitcast.4), custom_call_target="tpu_custom_call" | custom-call | tf_op jit(solution)/shard_map/pallas_call | solution.py:342
  86.0 7.8 %shard_map.56 = bf16[768,768]{1,0:T(8,128)(2,1)} custom-call(s32[1]{0:T(128)S(6)} %convert_element_type.3.owned_ref, f32[768,768]{1,0:T(8,128)S(1)} %get-tuple-element.7.base_ref, bf16[768,768]{1,0:T(8,128)(2,1)S(1)} %get-tuple-element.8.hot_ref), custom_call_target="tpu_custom_call" | custom-call | tf_op jit(solution)/shard_map/pallas_call | solution.py:378
